TPU v7x, 256 devices: a whole 4x4x8 slice. The times are simulated.
256 devices in a mesh: freq: 8 (over y_lo, x), ma: 32 (over z, y_hi, core).
Axes of the slice: x: 4, y: 4 (y_hi: 2, y_lo: 2; y = y_hi * 2 + y_lo), z: 8, core: 2. Of those that a mesh axis runs over, the one named last changes fastest.
Arguments:
- visibility: bfloat16 [8, 2048, 2, 1024], P('freq', 'ma'), may hold values from -6 to 6
- beam_blocks: bfloat16 [8, 64, 2, 1024, 1024], P('freq', 'ma'), may hold values from -0.1875 to 0.1875
- legendre: bfloat16 [64, 1024, 1024], P('ma'), may hold values from -0.1875 to 0.1875
- m_table: int32 [64], replicated, may hold values from 0 to 63, each once
- mode_counts: int32 [64], replicated, may hold values from 256 to 1024, as said below
- moment_weights: float32 [3, 8], replicated, may hold values from -2 to 2
Outputs:
- moments: float32 [3, 1024, 2048], P(None, 'ma', 'freq')
Inputs may be any that keep to these rules, and one draw needn't show every extreme that they name: `m_table`: each m of 0 to 63 stands in exactly one slot. `mode_counts`: m = 0 keeps all 1024 modes.
All inputs are finite; a program needn't handle non-finite values.
Results may differ from a plain program's by a relative error of at most 0.0041.
Values may be sent and summed in bfloat16 or wider, within the bound.
No kernel may reach another device: no remote copies, remote signals or barrier semaphores. Data moves between devices by JAX's collectives and lax.ppermute only.
A program may use at most 64 MiB of HBM per device.

v0:
```python
import functools
import math

import jax
import jax.numpy as jnp
from jax import lax
from jax.experimental import pallas as pl
from jax.experimental.pallas import tpu as pltpu
from jax.sharding import Mesh
from jax.sharding import PartitionSpec as P

f32, bf16, i32 = jnp.float32, jnp.bfloat16, jnp.int32
f16 = jnp.float16
LIFT = 32.0
PIECES = 4
HEADS = 4
SWAP = [(0, 1), (1, 0)]
CIRCLE = 2048
VMEM = pl.BlockSpec(memory_space=pltpu.VMEM)
ANY = pl.BlockSpec(memory_space=pl.ANY)
SMEM = pl.BlockSpec(memory_space=pltpu.SMEM)


def own_place():
    return lax.axis_index("chip") * 2 + lax.axis_index("core")


def iota(shape, dim):
    return lax.broadcasted_iota(i32, shape, dim)


def cos_of_index(index):
    folded = jnp.abs((index & (CIRCLE - 1)) - CIRCLE // 2) - CIRCLE // 4
    x = folded.astype(f32) * f32(2.0 * math.pi / CIRCLE)
    y = x * x
    poly = f32(1.0 / math.factorial(13))
    for n in (11, 9, 7, 5, 3):
        poly = poly * y + f32((-1.0) ** (n // 2) / math.factorial(n))
    return x + x * y * poly


def select_m(m_ref, slots):
    lanes = iota((slots.shape[0], m_ref.shape[1]), 1)
    return jnp.sum(jnp.where(lanes == slots, m_ref[...], 0).astype(f32), axis=1, keepdims=True).astype(i32)


def split(x):
    high = x.astype(bf16)
    return high, (x - high.astype(f32)).astype(bf16)


def time_table(m_ref, table_ref, time_local):
    place = own_place()
    rows, columns = table_ref.shape[0] // 2, table_ref.shape[1] // 2
    m_rows = select_m(m_ref, iota((rows, 1), 0) >> 1)
    out_part = iota((rows, columns), 0) & 1
    column = iota((rows, columns), 1)
    quarter = ((column & 1) - out_part) * (CIRCLE // 4)
    for other in range(2):
        first = (place ^ other) * time_local
        values = cos_of_index(m_rows * (first + (column >> 1)) - quarter)
        high, low = split(values)
        where = slice(other * columns, (other + 1) * columns)
        table_ref[:rows, where] = high
        table_ref[rows:, where] = low


def transform_kernel(table_ref, own_ref, other_ref, out_ref):
    rows, half = out_ref.shape
    place = pl.ds(pl.multiple_of(lax.axis_index("core") * half, half), half)
    other = other_ref[:, :, place].reshape(own_ref.shape[0], half)
    both = jnp.concatenate([own_ref[:, place], other], axis=0)
    total = jnp.dot(table_ref[...], both, preferred_element_type=f32)
    out_ref[...] = (total[:rows] + total[rows:]) * f32(LIFT)


def prepare_kernel(
    m_hbm, count_hbm, weight_hbm, m_line_hbm, own_hbm, beam_hbm,
    head_ref, own_ref, mode_ref, degree_ref, table_ref, spread_ref, line_ref,
    m_ref, count_ref, weight_ref, own, small_sems, sems, *, norm, time_local
):
    small = [
        pltpu.make_async_copy(source, target, small_sems.at[n])
        for n, (source, target) in enumerate(
            (
                (m_line_hbm, line_ref),
                (own_hbm, own),
                (m_hbm, m_ref),
                (count_hbm, count_ref),
                (weight_hbm, weight_ref),
            )
        )
    ]
    rows = head_ref.shape[1]
    heads = [
        pltpu.make_async_copy(
            beam_hbm.at[j // PIECES, pl.ds(j % PIECES * rows, rows)], head_ref.at[j], sems.at[j]
        )
        for j in range(head_ref.shape[0])
    ]
    for copy in small + heads:
        copy.start()
    small[0].wait()
    time_table(line_ref, table_ref, time_local)
    small[1].wait()
    own_ref[...] = own[...].reshape(own_ref.shape)
    for copy in small[2:]:
        copy.wait()
    place = own_place()
    slots = mode_ref.shape[0] // 2
    m_own = [m_ref[place * slots + j] for j in range(slots)]
    shape = mode_ref.shape
    counts = jnp.zeros(shape, i32)
    for j in range(slots):
        counts = jnp.where(iota(shape, 0) >> 1 == j, count_ref[m_own[j]], counts)
    mode_ref[...] = jnp.where(iota(shape, 1) < counts, f32(norm), f32(0.0))
    shape = degree_ref.shape
    firsts = jnp.zeros(shape, i32)
    for j in range(slots):
        firsts = jnp.where(iota(shape, 0) >> 1 == j, m_own[j], firsts)
    degree_ref[...] = jnp.where(iota(shape, 1) >= firsts, f32(1.0), f32(0.0))
    for k in range(weight_ref.shape[0]):
        for f in range(weight_ref.shape[1]):
            spread_ref[k, f : f + 1, :] = jnp.full((1, 128), weight_ref[k, f], f32)
    for copy in heads:
        copy.wait()


def azimuth_table(m_ref, table_ref):
    rows, pixels = table_ref.shape[1:]
    row = iota((rows, 1), 0)
    m_rows = select_m(m_ref, 2 * (row & 31) + (row >> 6))
    weights = jnp.where(m_rows == 0, 1.0, 2.0).astype(f32) * f32(1.0 / math.sqrt(rows))
    first = lax.axis_index("freq") * pixels
    index = m_rows * (first + iota((rows, pixels), 1)) + ((row >> 5) & 1) * (CIRCLE // 4)
    table_ref[0], table_ref[1] = split(cos_of_index(index) * weights)


def contract_kernel(
    parts_ref, mode_ref, degree_ref, line_ref, head_ref, beam_hbm, legendre_hbm,
    out_ref, swap_ref, azimuth_ref, sums, beam, legendre, sems
):
    heads, rows = head_ref.shape[:2]
    slots = legendre_hbm.shape[0]
    pieces = [
        (False, 2 * j + d, part) for j in range(slots) for d in range(2) for part in range(PIECES)
    ][heads:]
    for j in range(slots):
        after = [n for n, piece in enumerate(pieces) if not piece[0] and piece[1] < 2 * (j + 1)]
        pieces[after[-1] + 1 : after[-1] + 1] = [(True, j, part) for part in range(PIECES)]
    copies = {}
    for n, piece in enumerate(pieces):
        is_legendre, j, part = piece
        source, target = (legendre_hbm, legendre) if is_legendre else (beam_hbm, beam)
        place = pl.ds(part * rows, rows)
        copies[piece] = pltpu.make_async_copy(source.at[j, place], target.at[j, place], sems.at[n])
        copies[piece].start()
    azimuth_table(line_ref, azimuth_ref)

    def product(left, is_legendre, j):
        total = None
        for part in range(PIECES):
            place = slice(part * rows, (part + 1) * rows)
            piece = (is_legendre, j, part)
            if piece in copies:
                copies[piece].wait()
                block = (legendre if is_legendre else beam)[j, place, :]
            else:
                block = head_ref[j * PIECES + part]
            term = jnp.dot(left[:, place], block, preferred_element_type=f32)
            total = term if total is None else total + term
        return total

    halves = []
    for core in range(2):
        total = parts_ref[core]
        for source in range(core + 2, parts_ref.shape[0], 2):
            total = total + parts_ref[source]
        halves.append(total)
    spectra = (jnp.concatenate(halves, axis=1) * mode_ref[...]).astype(bf16)
    cycles = legendre.shape[2]
    for j in range(slots):
        with_real = product(spectra, False, 2 * j)
        with_imag = product(spectra, False, 2 * j + 1)
        re, im = 2 * j, 2 * j + 1
        coeffs = jnp.concatenate(
            [
                with_real[re : re + 1] + with_imag[im : im + 1],
                with_real[im : im + 1] - with_imag[re : re + 1],
            ],
            axis=0,
        )
        cycle = product((coeffs * degree_ref[re : re + 2, :]).astype(bf16), True, j)
        for c in range(2):
            for g in range(cycles // 128):
                sums[2 * j + c, pl.ds(g, 1), :] = cycle[c : c + 1, g * 128 : (g + 1) * 128]
    block = iota((cycles // 128, 128), 1) >> 5
    values = []
    for a in range(4):
        value = sums[0] if a == 0 else pltpu.roll(sums[0], 128 - 32 * a, 1)
        for q in range(1, 4):
            moved = sums[q] if a == q else pltpu.roll(sums[q], (32 * (q - a)) % 128, 1)
            value = jnp.where(block == q, moved, value)
        values.append(value)
    core = lax.axis_index("core")
    for half in range(2):
        even, odd = values[2 * half], values[2 * half + 1]
        chips = pl.ds(half, cycles // 128, stride=2)
        out_ref[chips, :] = jnp.where(core == 0, even, odd)
        swap_ref[chips, :] = jnp.where(core == 0, odd, even)


def synthesis_kernel(spread_ref, sums_ref, azimuth_ref, out_ref):
    moments, cycles, _ = out_ref.shape
    freqs = spread_ref.shape[1]
    owners = sums_ref.shape[0] // freqs
    blocks = [sums_ref[f * owners : (f + 1) * owners, :].astype(f32) for f in range(freqs)]
    turned = []
    for k in range(moments):
        total = spread_ref[k, 0:1, :] * blocks[0]
        for f in range(1, freqs):
            total = total + spread_ref[k, f : f + 1, :] * blocks[f]
        flipped = total.T
        turned.append(
            jnp.concatenate([flipped[q * cycles : (q + 1) * cycles] for q in range(4)], axis=1)
        )
    high, low = split(jnp.concatenate(turned, axis=0))
    out = (
        jnp.dot(high, azimuth_ref[0], preferred_element_type=f32)
        + jnp.dot(high, azimuth_ref[1], preferred_element_type=f32)
        + jnp.dot(low, azimuth_ref[0], preferred_element_type=f32)
    )
    for k in range(moments):
        out_ref[k] = out[k * cycles : (k + 1) * cycles]


def params(mib):
    return pltpu.CompilerParams(vmem_limit_bytes=mib << 20)


def local(visibility, beam_blocks, legendre, m_table, mode_counts, moment_weights):
    time_local, modes = visibility.shape[1], visibility.shape[3]
    places = lax.axis_size("chip") * lax.axis_size("core")
    freqs = lax.axis_size("freq")
    total_time = time_local * places
    slots_all = m_table.shape[0]
    slots = slots_all // places
    cycles = legendre.shape[2]
    moments = moment_weights.shape[0]
    depth = 2 * time_local

    other = lax.ppermute(visibility, "core", SWAP)
    beam, degrees = beam_blocks.reshape(2 * slots, modes, -1), beam_blocks.shape[4]
    rows = modes // PIECES
    head, own, mode_mask, degree_mask, table, spread, line = pl.pallas_call(
        functools.partial(prepare_kernel, norm=1.0 / (LIFT * math.sqrt(total_time)), time_local=time_local),
        out_shape=(
            pltpu.VMEM((HEADS, rows, degrees), bf16),
            pltpu.VMEM((depth, modes), bf16),
            pltpu.VMEM((2 * slots, modes), f32),
            pltpu.VMEM((2 * slots, degrees), f32),
            pltpu.VMEM((4 * slots_all, 2 * depth), bf16),
            pltpu.VMEM((moments, freqs, 128), f32),
            pltpu.VMEM((1, slots_all), i32),
        ),
        in_specs=[ANY] * 6,
        out_specs=(VMEM,) * 7,
        scratch_shapes=[
            pltpu.SMEM(m_table.shape, i32),
            pltpu.SMEM(mode_counts.shape, i32),
            pltpu.SMEM(moment_weights.shape, f32),
            pltpu.VMEM((time_local, 2, modes), bf16),
            pltpu.SemaphoreType.DMA((5,)),
            pltpu.SemaphoreType.DMA((HEADS,)),
        ],
        compiler_params=params(54),
        name="prepare",
    )(m_table, mode_counts, moment_weights, m_table[None, :], visibility[0], beam)
    parts = pl.pallas_call(
        transform_kernel,
        out_shape=jax.ShapeDtypeStruct((2 * slots_all, modes // 2), f32),
        in_specs=[VMEM, VMEM, VMEM],
        out_specs=VMEM,
        compiler_params=params(16),
        name="transform",
    )(table, own, other[0])
    parts = lax.all_to_all(
        parts.reshape(places, 2 * slots, modes // 2).astype(f16), ("chip", "core"), split_axis=0, concat_axis=0
    ).astype(f32)
    sums, swapped, azimuth = pl.pallas_call(
        contract_kernel,
        out_shape=(
            pltpu.VMEM((places // 2, 128), f32),
            pltpu.VMEM((places // 2, 128), f32),
            pltpu.VMEM((2, 2 * slots_all, CIRCLE // freqs), bf16),
        ),
        in_specs=[VMEM, VMEM, VMEM, VMEM, VMEM, ANY, ANY],
        out_specs=(VMEM, VMEM, VMEM),
        scratch_shapes=[
            pltpu.VMEM((2 * slots, cycles // 128, 128), f32),
            pltpu.VMEM(beam.shape, bf16),
            pltpu.VMEM(legendre.shape, bf16),
            pltpu.SemaphoreType.DMA((3 * slots * PIECES - HEADS,)),
        ],
        compiler_params=params(48),
        name="contract",
    )(parts, mode_mask, degree_mask, line, head, beam, legendre)
    swapped = lax.ppermute(swapped, "core", SWAP)
    first = lax.axis_index("core") == 0
    pair = jnp.stack(
        [jnp.where(first, sums, swapped), jnp.where(first, swapped, sums)], axis=1
    ).astype(bf16)
    sums = lax.all_to_all(
        jnp.broadcast_to(pair[None], (freqs,) + pair.shape).reshape((-1,) + pair.shape[1:]),
        ("freq", "chip"),
        split_axis=0,
        concat_axis=0,
    ).reshape(freqs * places, 128)
    return pl.pallas_call(
        synthesis_kernel,
        out_shape=jax.ShapeDtypeStruct((moments, cycles // places, CIRCLE // freqs), f32),
        in_specs=[VMEM, VMEM, VMEM],
        out_specs=VMEM,
        compiler_params=params(16),
        name="synthesis",
    )(spread, sums, azimuth)


def solution(mesh):
    freqs, places = mesh.devices.shape
    fine = Mesh(mesh.devices.reshape(freqs, places // 2, 2), ("freq", "chip", "core"))
    ma = ("chip", "core")
    placed = (
        P("freq", ma, None, None),
        P("freq", ma, None, None, None),
        P(ma, None, None),
        P(),
        P(),
        P(),
    )
    return jax.shard_map(
        local, mesh=fine, in_specs=placed, out_specs=P(None, ma, "freq"), check_vma=False
    )
```

profile of v0, /device:TPU:1, one launch (start us, length us, event | category | flops | bytes accessed | tf_op | source)
XLA Modules:
  0.0 49.8 jit_solution(8764088242320158606)
XLA Ops:
  0.0 3.2 %collective-permute-start = (bf16[1,64,2,1024]{3,2,1,0:T(2,128)(2,1)}, bf16[1,64,2,1024]{3,2,1,0:T(2,128)(2,1)S(1)}, u32[]{:S(2)}, u32[]{:S(2)}) collective-permute-start(bf16[1,64,2,1024]{3,2,1,0:T(2,128)(2,1)} %param.6), channel_id=1, source_target_pairs={{0,1},{1,0},{2,3},{3,2},{4,5},{5,4},{6,7},{7,6},{8,9},{9,8},{10,11... | collective-permute-start | bytes 786440 | tf_op jit(solution)/shard_map/ppermute | solution.py:252
  3.2 1.7 %prepare.1 = (bf16[4,256,1024]{2,1,0:T(8,128)(2,1)S(1)}, bf16[128,1024]{1,0:T(8,128)(2,1)S(1)}, f32[4,1024]{1,0:T(4,128)S(1)}, f32[4,1024]{1,0:T(4,128)S(1)}, bf...) custom-call(s32[64]{0:T(128)} %m_hbm.1, s32[64]{0:T(128)} %count_hbm.1, ...), custom_call_target="tpu_custom_call" | custom-call | tf_op jit(solution)/shard_map/prepare/pallas_call | solution.py:255
  4.9 0.0 collective-permute-done
  4.9 0.2 transform.1
  5.3 20.2 %all_to_all.10 = f16[32,4,512]{2,1,0:T(4,128)(2,1)S(1)} all-to-all(f16[32,4,512]{2,1,0:T(4,128)(2,1)S(1)} %convert_element_type.15), channel_id=1, replica_groups=mesh['freq'=8,'chip'=16,'core'=2] {'chip','core'}, dimensions={0} | all-to-all | bytes 262144 | tf_op jit(solution)/shard_map/all_to_all | solution.py:287
  25.5 4.5 %contract.1 = (f32[16,128]{1,0:T(8,128)S(1)}, f32[16,128]{1,0:T(8,128)S(1)}, bf16[2,128,256]{2,1,0:T(8,128)(2,1)S(1)}) custom-call(f32[32,4,512]{2,1,0:T(4,128)S(1)} %convert_element_type.16.parts_ref, f32[4,1024]{1,0:T(4,128)S(1)} %get-tuple-element.18.mode_ref, f32[4,1024]{1,0:T(4,128)S(1)} %get-tuple-element.19.degree_ref, ...), custom_call_target="tpu_custom_call" | custom-call | tf_op jit(solution)/shard_map/contract/pallas_call | solution.py:290
  30.0 0.3 collective-permute-start.1
  30.4 0.9 %collective-permute-done.1 = bf16[16,128]{1,0:T(8,128)(2,1)S(1)} collective-permute-done((bf16[16,128]{1,0:T(8,128)(2,1)S(1)}, bf16[16,128]{1,0:T(8,128)(2,1)S(1)}, u32[]{:S(2)}, u32[]{:S(2)}) %collective-permute-start.1) | collective-permute-done | bytes 4128 | tf_op jit(solution)/shard_map/ppermute | solution.py:308
  31.4 17.4 %all_to_all.11 = bf16[128,2,128]{2,1,0:T(2,128)(2,1)S(1)} all-to-all(bf16[128,2,128]{2,1,0:T(2,128)(2,1)S(1)} %bitcast.14), channel_id=1, replica_groups=mesh['freq'=8,'chip'=16,'core'=2] {'freq','chip'}, dimensions={0} | all-to-all | bytes 131072 | tf_op jit(solution)/shard_map/all_to_all | solution.py:313
  48.8 1.0 %synthesis.1 = f32[3,32,256]{2,1,0:T(8,128)} custom-call(f32[3,8,128]{2,1,0:T(8,128)S(1)} %get-tuple-element.15.spread_ref, bf16[256,128]{1,0:T(8,128)(2,1)S(1)} %bitcast.11, bf16[2,128,256]{2,1,0:T(8,128)(2,1)S(1)} %get-tuple-element.24.azimuth_ref), custom_call_target="tpu_custom_call" | custom-call | tf_op jit(solution)/shard_map/synthesis/pallas_call | solution.py:319
  (8 shorter events, 0.2 us)
Async XLA Ops:
  0.0 4.9 %collective-permute-start = (bf16[1,64,2,1024]{3,2,1,0:T(2,128)(2,1)}, bf16[1,64,2,1024]{3,2,1,0:T(2,128)(2,1)S(1)}, u32[]{:S(2)}, u32[]{:S(2)}) collective-permute-start(bf16[1,64,2,1024]{3,2,1,0:T(2,128)(2,1)} %param.6), channel_id=1, source_target_pairs={{0,1},{1,0},{2,3},{3,2},{4,5},{5,4},{6,7},{7,6},{8,9},{9,8},{10,11... | collective-permute-start | bytes 786440 | tf_op jit(solution)/shard_map/ppermute | solution.py:252
  30.0 1.3 %collective-permute-start.1 = (bf16[16,128]{1,0:T(8,128)(2,1)S(1)}, bf16[16,128]{1,0:T(8,128)(2,1)S(1)}, u32[]{:S(2)}, u32[]{:S(2)}) collective-permute-start(bf16[16,128]{1,0:T(8,128)(2,1)S(1)} %convert.16), channel_id=1, source_target_pairs={{0,1},{1,0},{2,3},{3,2},{4,5},{5,4},{6,7},{7,6},{8,9},{9,8},{10,11... | collective-permute-start | bytes 12296 | tf_op jit(solution)/shard_map/ppermute | solution.py:308
where the time goes:
time: 50 us; the launch traced here: 49.8 us
  blocking collectives  37.6 us (75%)
  Pallas kernels  7.43 us (15%)
  starting transfers between devices  3.56 us (7%)
  waiting for transfers between devices  0.94 us (2%)
    all_to_all x1, blocking collectives, local(): lax.all_to_all(parts.reshape(places, 2 * slots, modes // 2).astype(f16),...  20.2 us
    all_to_all x1, blocking collectives, local(): lax.all_to_all(jnp.broadcast_to(pair[None], (freqs,) + pair.shape).reshap...  17.4 us
    pallas_call x1, Pallas kernels, local(): pl.pallas_call(contract_kernel, out_shape=(pltpu.VMEM((places // 2, 128),...  4.5 us
    ppermute x1, starting transfers between devices, local(): other = lax.ppermute(visibility, 'core', SWAP)  3.24 us
    pallas_call x1, Pallas kernels, local(): pl.pallas_call(functools.partial(prepare_kernel, norm=1.0 / (LIFT * math....  1.69 us
    pallas_call x1, Pallas kernels, local(): pl.pallas_call(synthesis_kernel, out_shape=jax.ShapeDtypeStruct((moments,...  1 us
  transfers between devices with their start and end apart: 2, of which 1 were waited for; matrix products, arithmetic and copies ran while one was open for 0% of the time, Pallas kernels for 3%

commit v1 on v0

--- a/solution.py
+++ b/solution.py
@@ -49,29 +49,25 @@
     return high, (x - high.astype(f32)).astype(bf16)
 
 
-def time_table(m_ref, table_ref, time_local):
-    place = own_place()
-    rows, columns = table_ref.shape[0] // 2, table_ref.shape[1] // 2
-    m_rows = select_m(m_ref, iota((rows, 1), 0) >> 1)
-    out_part = iota((rows, columns), 0) & 1
-    column = iota((rows, columns), 1)
-    quarter = ((column & 1) - out_part) * (CIRCLE // 4)
-    for other in range(2):
-        first = (place ^ other) * time_local
-        values = cos_of_index(m_rows * (first + (column >> 1)) - quarter)
-        high, low = split(values)
-        where = slice(other * columns, (other + 1) * columns)
-        table_ref[:rows, where] = high
-        table_ref[rows:, where] = low
+def time_table(m_ref, shape, time_local, other):
+    m_rows = select_m(m_ref, iota((shape[0], 1), 0) >> 1)
+    column = iota(shape, 1)
+    quarter = ((column & 1) - (iota(shape, 0) & 1)) * (CIRCLE // 4)
+    first = (own_place() ^ other) * time_local
+    return jnp.concatenate(split(cos_of_index(m_rows * (first + (column >> 1)) - quarter)), axis=0)
+
+
+def half_transform(table, block_ref):
+    rows, depth = table.shape[0] // 2, table.shape[1]
+    half = block_ref.shape[2] // 2
+    place = pl.ds(pl.multiple_of(lax.axis_index("core") * half, half), half)
+    block = block_ref[:, :, place].reshape(depth, half)
+    total = jnp.dot(table, block, preferred_element_type=f32)
+    return (total[:rows] + total[rows:]) * f32(LIFT)
 
 
 def transform_kernel(table_ref, own_ref, other_ref, out_ref):
-    rows, half = out_ref.shape
-    place = pl.ds(pl.multiple_of(lax.axis_index("core") * half, half), half)
-    other = other_ref[:, :, place].reshape(own_ref.shape[0], half)
-    both = jnp.concatenate([own_ref[:, place], other], axis=0)
-    total = jnp.dot(table_ref[...], both, preferred_element_type=f32)
-    out_ref[...] = (total[:rows] + total[rows:]) * f32(LIFT)
+    out_ref[...] = own_ref[...] + half_transform(table_ref[...], other_ref)
 
 
 def prepare_kernel(
@@ -98,12 +94,14 @@
         )
         for j in range(head_ref.shape[0])
     ]
-    for copy in small + heads:
+    for copy in small[:1] + heads + small[1:]:
         copy.start()
     small[0].wait()
-    time_table(line_ref, table_ref, time_local)
+    shape = table_ref.shape[0] // 2, table_ref.shape[1]
+    table_ref[...] = time_table(line_ref, shape, time_local, 1)
+    table = time_table(line_ref, shape, time_local, 0)
     small[1].wait()
-    own_ref[...] = own[...].reshape(own_ref.shape)
+    own_ref[...] = half_transform(table, own)
     for copy in small[2:]:
         copy.wait()
     place = own_place()
@@ -157,8 +155,7 @@
         copies[piece].start()
     azimuth_table(line_ref, azimuth_ref)
 
-    def product(left, is_legendre, j):
-        total = None
+    def product(left, is_legendre, j, total=None):
         for part in range(PIECES):
             place = slice(part * rows, (part + 1) * rows)
             piece = (is_legendre, j, part)
@@ -177,23 +174,20 @@
         for source in range(core + 2, parts_ref.shape[0], 2):
             total = total + parts_ref[source]
         halves.append(total)
-    spectra = (jnp.concatenate(halves, axis=1) * mode_ref[...]).astype(bf16)
+    spectra = jnp.concatenate(halves, axis=1) * mode_ref[...]
+    turned = []
+    for j in range(slots):
+        turned += [spectra[2 * j + 1 : 2 * j + 2], -spectra[2 * j : 2 * j + 1]]
+    turned = jnp.concatenate(turned, axis=0).astype(bf16)
+    spectra = spectra.astype(bf16)
     cycles = legendre.shape[2]
     for j in range(slots):
-        with_real = product(spectra, False, 2 * j)
-        with_imag = product(spectra, False, 2 * j + 1)
-        re, im = 2 * j, 2 * j + 1
-        coeffs = jnp.concatenate(
-            [
-                with_real[re : re + 1] + with_imag[im : im + 1],
-                with_real[im : im + 1] - with_imag[re : re + 1],
-            ],
-            axis=0,
-        )
-        cycle = product((coeffs * degree_ref[re : re + 2, :]).astype(bf16), True, j)
+        coeffs = product(spectra, False, 2 * j)
+        coeffs = product(turned, False, 2 * j + 1, coeffs)
+        cycle = product((coeffs * degree_ref[...]).astype(bf16), True, j)
         for c in range(2):
             for g in range(cycles // 128):
-                sums[2 * j + c, pl.ds(g, 1), :] = cycle[c : c + 1, g * 128 : (g + 1) * 128]
+                sums[2 * j + c, pl.ds(g, 1), :] = cycle[2 * j + c : 2 * j + c + 1, g * 128 : (g + 1) * 128]
     block = iota((cycles // 128, 128), 1) >> 5
     values = []
     for a in range(4):
@@ -256,10 +250,10 @@
         functools.partial(prepare_kernel, norm=1.0 / (LIFT * math.sqrt(total_time)), time_local=time_local),
         out_shape=(
             pltpu.VMEM((HEADS, rows, degrees), bf16),
-            pltpu.VMEM((depth, modes), bf16),
+            pltpu.VMEM((2 * slots_all, modes // 2), f32),
             pltpu.VMEM((2 * slots, modes), f32),
             pltpu.VMEM((2 * slots, degrees), f32),
-            pltpu.VMEM((4 * slots_all, 2 * depth), bf16),
+            pltpu.VMEM((4 * slots_all, depth), bf16),
             pltpu.VMEM((moments, freqs, 128), f32),
             pltpu.VMEM((1, slots_all), i32),
         ),

time: 50 us -> 49.9 us (level)
  no operation moved by 1% of the time
where the time goes in v1:
time: 49.9 us; the launch traced here: 49.7 us
  blocking collectives  37.6 us (75%)
  Pallas kernels  7.37 us (15%)
  starting transfers between devices  3.56 us (7%)
  waiting for transfers between devices  0.94 us (2%)
    all_to_all x1, blocking collectives, local(): lax.all_to_all(parts.reshape(places, 2 * slots, modes // 2).astype(f16),...  20.2 us
    all_to_all x1, blocking collectives, local(): lax.all_to_all(jnp.broadcast_to(pair[None], (freqs,) + pair.shape).reshap...  17.4 us
    pallas_call x1, Pallas kernels, local(): pl.pallas_call(contract_kernel, out_shape=(pltpu.VMEM((places // 2, 128),...  4.46 us
    ppermute x1, starting transfers between devices, local(): other = lax.ppermute(visibility, 'core', SWAP)  3.24 us
    pallas_call x1, Pallas kernels, local(): pl.pallas_call(functools.partial(prepare_kernel, norm=1.0 / (LIFT * math....  1.69 us
    pallas_call x1, Pallas kernels, local(): pl.pallas_call(synthesis_kernel, out_shape=jax.ShapeDtypeStruct((moments,...  1 us
  transfers between devices with their start and end apart: 2, of which 1 were waited for; matrix products, arithmetic and copies ran while one was open for 0% of the time, Pallas kernels for 3%

profile of v1, /device:TPU:1, one launch (start us, length us, event | category | flops | bytes accessed | tf_op | source)
XLA Modules:
  0.0 49.7 jit_solution(11706676997184719285)
XLA Ops:
  0.0 3.2 %collective-permute-start = (bf16[1,64,2,1024]{3,2,1,0:T(2,128)(2,1)}, bf16[1,64,2,1024]{3,2,1,0:T(2,128)(2,1)S(1)}, u32[]{:S(2)}, u32[]{:S(2)}) collective-permute-start(bf16[1,64,2,1024]{3,2,1,0:T(2,128)(2,1)} %param.6), channel_id=1, source_target_pairs={{0,1},{1,0},{2,3},{3,2},{4,5},{5,4},{6,7},{7,6},{8,9},{9,8},{10,11... | collective-permute-start | bytes 786440 | tf_op jit(solution)/shard_map/ppermute | solution.py:246
  3.2 1.7 %prepare.1 = (bf16[4,256,1024]{2,1,0:T(8,128)(2,1)S(1)}, f32[128,512]{1,0:T(8,128)S(1)}, f32[4,1024]{1,0:T(4,128)S(1)}, f32[4,1024]{1,0:T(4,128)S(1)}, bf16[256,...) custom-call(s32[64]{0:T(128)} %m_hbm.1, s32[64]{0:T(128)} %count_hbm.1, f32[3,8]{1,0:T(4,128)} %weight_hbm.1, ...), custom_call_target="tpu_custom_call" | custom-call | tf_op jit(solution)/shard_map/prepare/pallas_call | solution.py:249
  4.9 0.0 collective-permute-done
  4.9 0.2 transform.1
  5.3 20.2 %all_to_all.10 = f16[32,4,512]{2,1,0:T(4,128)(2,1)S(1)} all-to-all(f16[32,4,512]{2,1,0:T(4,128)(2,1)S(1)} %convert_element_type.15), channel_id=1, replica_groups=mesh['freq'=8,'chip'=16,'core'=2] {'chip','core'}, dimensions={0} | all-to-all | bytes 262144 | tf_op jit(solution)/shard_map/all_to_all | solution.py:281
  25.5 4.5 %contract.1 = (f32[16,128]{1,0:T(8,128)S(1)}, f32[16,128]{1,0:T(8,128)S(1)}, bf16[2,128,256]{2,1,0:T(8,128)(2,1)S(1)}) custom-call(f32[32,4,512]{2,1,0:T(4,128)S(1)} %convert_element_type.16.parts_ref, f32[4,1024]{1,0:T(4,128)S(1)} %get-tuple-element.18.mode_ref, f32[4,1024]{1,0:T(4,128)S(1)} %get-tuple-element.19.degree_ref, ...), custom_call_target="tpu_custom_call" | custom-call | tf_op jit(solution)/shard_map/contract/pallas_call | solution.py:284
  30.0 0.3 collective-permute-start.1
  30.3 0.9 %collective-permute-done.1 = bf16[16,128]{1,0:T(8,128)(2,1)S(1)} collective-permute-done((bf16[16,128]{1,0:T(8,128)(2,1)S(1)}, bf16[16,128]{1,0:T(8,128)(2,1)S(1)}, u32[]{:S(2)}, u32[]{:S(2)}) %collective-permute-start.1) | collective-permute-done | bytes 4128 | tf_op jit(solution)/shard_map/ppermute | solution.py:302
  31.3 17.4 %all_to_all.11 = bf16[128,2,128]{2,1,0:T(2,128)(2,1)S(1)} all-to-all(bf16[128,2,128]{2,1,0:T(2,128)(2,1)S(1)} %bitcast.14), channel_id=1, replica_groups=mesh['freq'=8,'chip'=16,'core'=2] {'freq','chip'}, dimensions={0} | all-to-all | bytes 131072 | tf_op jit(solution)/shard_map/all_to_all | solution.py:307
  48.7 1.0 %synthesis.1 = f32[3,32,256]{2,1,0:T(8,128)} custom-call(f32[3,8,128]{2,1,0:T(8,128)S(1)} %get-tuple-element.15.spread_ref, bf16[256,128]{1,0:T(8,128)(2,1)S(1)} %bitcast.10, bf16[2,128,256]{2,1,0:T(8,128)(2,1)S(1)} %get-tuple-element.24.azimuth_ref), custom_call_target="tpu_custom_call" | custom-call | tf_op jit(solution)/shard_map/synthesis/pallas_call | solution.py:313
  (8 shorter events, 0.2 us)
Async XLA Ops:
  0.0 4.9 %collective-permute-start = (bf16[1,64,2,1024]{3,2,1,0:T(2,128)(2,1)}, bf16[1,64,2,1024]{3,2,1,0:T(2,128)(2,1)S(1)}, u32[]{:S(2)}, u32[]{:S(2)}) collective-permute-start(bf16[1,64,2,1024]{3,2,1,0:T(2,128)(2,1)} %param.6), channel_id=1, source_target_pairs={{0,1},{1,0},{2,3},{3,2},{4,5},{5,4},{6,7},{7,6},{8,9},{9,8},{10,11... | collective-permute-start | bytes 786440 | tf_op jit(solution)/shard_map/ppermute | solution.py:246
  30.0 1.3 %collective-permute-start.1 = (bf16[16,128]{1,0:T(8,128)(2,1)S(1)}, bf16[16,128]{1,0:T(8,128)(2,1)S(1)}, u32[]{:S(2)}, u32[]{:S(2)}) collective-permute-start(bf16[16,128]{1,0:T(8,128)(2,1)S(1)} %convert.16), channel_id=1, source_target_pairs={{0,1},{1,0},{2,3},{3,2},{4,5},{5,4},{6,7},{7,6},{8,9},{9,8},{10,11... | collective-permute-start | bytes 12296 | tf_op jit(solution)/shard_map/ppermute | solution.py:302

commit v2 on v0

--- a/solution.py
+++ b/solution.py
@@ -13,7 +13,7 @@
 f16 = jnp.float16
 LIFT = 32.0
 PIECES = 4
-HEADS = 4
+HEADS = 5
 SWAP = [(0, 1), (1, 0)]
 CIRCLE = 2048
 VMEM = pl.BlockSpec(memory_space=pltpu.VMEM)
@@ -98,7 +98,7 @@
         )
         for j in range(head_ref.shape[0])
     ]
-    for copy in small + heads:
+    for copy in small[:1] + heads + small[1:]:
         copy.start()
     small[0].wait()
     time_table(line_ref, table_ref, time_local)
@@ -157,8 +157,7 @@
         copies[piece].start()
     azimuth_table(line_ref, azimuth_ref)
 
-    def product(left, is_legendre, j):
-        total = None
+    def product(left, is_legendre, j, total=None):
         for part in range(PIECES):
             place = slice(part * rows, (part + 1) * rows)
             piece = (is_legendre, j, part)
@@ -177,23 +176,20 @@
         for source in range(core + 2, parts_ref.shape[0], 2):
             total = total + parts_ref[source]
         halves.append(total)
-    spectra = (jnp.concatenate(halves, axis=1) * mode_ref[...]).astype(bf16)
+    spectra = jnp.concatenate(halves, axis=1) * mode_ref[...]
+    turned = []
+    for j in range(slots):
+        turned += [spectra[2 * j + 1 : 2 * j + 2], -spectra[2 * j : 2 * j + 1]]
+    turned = jnp.concatenate(turned, axis=0).astype(bf16)
+    spectra = spectra.astype(bf16)
     cycles = legendre.shape[2]
     for j in range(slots):
-        with_real = product(spectra, False, 2 * j)
-        with_imag = product(spectra, False, 2 * j + 1)
-        re, im = 2 * j, 2 * j + 1
-        coeffs = jnp.concatenate(
-            [
-                with_real[re : re + 1] + with_imag[im : im + 1],
-                with_real[im : im + 1] - with_imag[re : re + 1],
-            ],
-            axis=0,
-        )
-        cycle = product((coeffs * degree_ref[re : re + 2, :]).astype(bf16), True, j)
+        coeffs = product(spectra, False, 2 * j)
+        coeffs = product(turned, False, 2 * j + 1, coeffs)
+        cycle = product((coeffs * degree_ref[...]).astype(bf16), True, j)
         for c in range(2):
             for g in range(cycles // 128):
-                sums[2 * j + c, pl.ds(g, 1), :] = cycle[c : c + 1, g * 128 : (g + 1) * 128]
+                sums[2 * j + c, pl.ds(g, 1), :] = cycle[2 * j + c : 2 * j + c + 1, g * 128 : (g + 1) * 128]
     block = iota((cycles // 128, 128), 1) >> 5
     values = []
     for a in range(4):

time: 50 us -> 50 us (level)
  transfers between devices with their start and end apart: 2 -> 2, of which waited for: 1 -> 1; matrix products, arithmetic and copies ran while one was open for 0% -> 0% of each run, Pallas kernels for 3% -> 4%
where the time goes in v2:
time: 50 us; the launch traced here: 49.9 us
  blocking collectives  37.6 us (75%)
  Pallas kernels  7.5 us (15%)
  starting transfers between devices  3.56 us (7%)
  waiting for transfers between devices  0.94 us (2%)
    all_to_all x1, blocking collectives, local(): lax.all_to_all(parts.reshape(places, 2 * slots, modes // 2).astype(f16),...  20.2 us
    all_to_all x1, blocking collectives, local(): lax.all_to_all(jnp.broadcast_to(pair[None], (freqs,) + pair.shape).reshap...  17.4 us
    pallas_call x1, Pallas kernels, local(): pl.pallas_call(contract_kernel, out_shape=(pltpu.VMEM((places // 2, 128),...  4.4 us
    ppermute x1, starting transfers between devices, local(): other = lax.ppermute(visibility, 'core', SWAP)  3.24 us
    pallas_call x1, Pallas kernels, local(): pl.pallas_call(functools.partial(prepare_kernel, norm=1.0 / (LIFT * math....  1.85 us
    pallas_call x1, Pallas kernels, local(): pl.pallas_call(synthesis_kernel, out_shape=jax.ShapeDtypeStruct((moments,...  1 us
  transfers between devices with their start and end apart: 2, of which 1 were waited for; matrix products, arithmetic and copies ran while one was open for 0% of the time, Pallas kernels for 4%

profile of v2, /device:TPU:1, one launch (start us, length us, event | category | flops | bytes accessed | tf_op | source)
XLA Modules:
  0.0 49.9 jit_solution(6831859304475676453)
XLA Ops:
  0.0 3.2 %collective-permute-start = (bf16[1,64,2,1024]{3,2,1,0:T(2,128)(2,1)}, bf16[1,64,2,1024]{3,2,1,0:T(2,128)(2,1)S(1)}, u32[]{:S(2)}, u32[]{:S(2)}) collective-permute-start(bf16[1,64,2,1024]{3,2,1,0:T(2,128)(2,1)} %param.6), channel_id=1, source_target_pairs={{0,1},{1,0},{2,3},{3,2},{4,5},{5,4},{6,7},{7,6},{8,9},{9,8},{10,11... | collective-permute-start | bytes 786440 | tf_op jit(solution)/shard_map/ppermute | solution.py:248
  3.2 1.9 %prepare.1 = (bf16[5,256,1024]{2,1,0:T(8,128)(2,1)S(1)}, bf16[128,1024]{1,0:T(8,128)(2,1)S(1)}, f32[4,1024]{1,0:T(4,128)S(1)}, f32[4,1024]{1,0:T(4,128)S(1)}, bf...) custom-call(s32[64]{0:T(128)} %m_hbm.1, s32[64]{0:T(128)} %count_hbm.1, ...), custom_call_target="tpu_custom_call" | custom-call | tf_op jit(solution)/shard_map/prepare/pallas_call | solution.py:251
  5.1 0.0 collective-permute-done
  5.1 0.2 transform.1
  5.4 20.2 %all_to_all.10 = f16[32,4,512]{2,1,0:T(4,128)(2,1)S(1)} all-to-all(f16[32,4,512]{2,1,0:T(4,128)(2,1)S(1)} %convert_element_type.15), channel_id=1, replica_groups=mesh['freq'=8,'chip'=16,'core'=2] {'chip','core'}, dimensions={0} | all-to-all | bytes 262144 | tf_op jit(solution)/shard_map/all_to_all | solution.py:283
  25.7 4.4 %contract.1 = (f32[16,128]{1,0:T(8,128)S(1)}, f32[16,128]{1,0:T(8,128)S(1)}, bf16[2,128,256]{2,1,0:T(8,128)(2,1)S(1)}) custom-call(f32[32,4,512]{2,1,0:T(4,128)S(1)} %convert_element_type.16.parts_ref, f32[4,1024]{1,0:T(4,128)S(1)} %get-tuple-element.18.mode_ref, f32[4,1024]{1,0:T(4,128)S(1)} %get-tuple-element.19.degree_ref, ...), custom_call_target="tpu_custom_call" | custom-call | tf_op jit(solution)/shard_map/contract/pallas_call | solution.py:286
  30.1 0.3 collective-permute-start.1
  30.4 0.9 %collective-permute-done.1 = bf16[16,128]{1,0:T(8,128)(2,1)S(1)} collective-permute-done((bf16[16,128]{1,0:T(8,128)(2,1)S(1)}, bf16[16,128]{1,0:T(8,128)(2,1)S(1)}, u32[]{:S(2)}, u32[]{:S(2)}) %collective-permute-start.1) | collective-permute-done | bytes 4128 | tf_op jit(solution)/shard_map/ppermute | solution.py:304
  31.4 17.4 %all_to_all.11 = bf16[128,2,128]{2,1,0:T(2,128)(2,1)S(1)} all-to-all(bf16[128,2,128]{2,1,0:T(2,128)(2,1)S(1)} %bitcast.14), channel_id=1, replica_groups=mesh['freq'=8,'chip'=16,'core'=2] {'freq','chip'}, dimensions={0} | all-to-all | bytes 131072 | tf_op jit(solution)/shard_map/all_to_all | solution.py:309
  48.9 1.0 %synthesis.1 = f32[3,32,256]{2,1,0:T(8,128)} custom-call(f32[3,8,128]{2,1,0:T(8,128)S(1)} %get-tuple-element.15.spread_ref, bf16[256,128]{1,0:T(8,128)(2,1)S(1)} %bitcast.11, bf16[2,128,256]{2,1,0:T(8,128)(2,1)S(1)} %get-tuple-element.24.azimuth_ref), custom_call_target="tpu_custom_call" | custom-call | tf_op jit(solution)/shard_map/synthesis/pallas_call | solution.py:315
  (8 shorter events, 0.2 us)
Async XLA Ops:
  0.0 5.1 %collective-permute-start = (bf16[1,64,2,1024]{3,2,1,0:T(2,128)(2,1)}, bf16[1,64,2,1024]{3,2,1,0:T(2,128)(2,1)S(1)}, u32[]{:S(2)}, u32[]{:S(2)}) collective-permute-start(bf16[1,64,2,1024]{3,2,1,0:T(2,128)(2,1)} %param.6), channel_id=1, source_target_pairs={{0,1},{1,0},{2,3},{3,2},{4,5},{5,4},{6,7},{7,6},{8,9},{9,8},{10,11... | collective-permute-start | bytes 786440 | tf_op jit(solution)/shard_map/ppermute | solution.py:248
  30.1 1.3 %collective-permute-start.1 = (bf16[16,128]{1,0:T(8,128)(2,1)S(1)}, bf16[16,128]{1,0:T(8,128)(2,1)S(1)}, u32[]{:S(2)}, u32[]{:S(2)}) collective-permute-start(bf16[16,128]{1,0:T(8,128)(2,1)S(1)} %convert.16), channel_id=1, source_target_pairs={{0,1},{1,0},{2,3},{3,2},{4,5},{5,4},{6,7},{7,6},{8,9},{9,8},{10,11... | collective-permute-start | bytes 12296 | tf_op jit(solution)/shard_map/ppermute | solution.py:304
